TPU v7x, 256 devices: a whole 4x4x8 slice. The times are simulated.
256 devices in a mesh: chan: 64 (over y, x_hi, z), seg: 4 (over x_lo, core).
Axes of the slice: x: 4 (x_hi: 2, x_lo: 2; x = x_hi * 2 + x_lo), y: 4, z: 8, core: 2. Of those that a mesh axis runs over, the one named last changes fastest.
Arguments:
- spectra: bfloat16 [4, 256, 4096], P('seg', 'chan'), may hold values from -6 to 6
- band_gain: float32 [2048], replicated, may hold values from 0.1 to 1
Outputs:
- correlations: float32 [256, 201, 256], P(('chan', 'seg'))
All inputs are finite; a program needn't handle non-finite values.
Results may differ from a plain program's by a relative error of at most 0.0003.
Values may be sent and summed in bfloat16 or wider, within the bound.
A program may use at most 64 MiB of HBM per device.

v0:
```python
import math

import jax
import jax.numpy as jnp
from jax import lax
from jax.sharding import PartitionSpec as P

MAXLAG = 100


def make_table(band_gain):
    half = band_gain.shape[0]
    bins = jnp.arange(half, dtype=jnp.int32)[:, None]
    lag_steps = jnp.arange(2 * MAXLAG + 1, dtype=jnp.int32)[None, :] - MAXLAG
    phase_index = jnp.mod(bins * lag_steps, 2 * half)
    angles = 2.0 * math.pi / (2 * half) * phase_index.astype(jnp.float32)
    weights = band_gain[:, None] / math.sqrt(half)
    return jnp.concatenate([weights * jnp.cos(angles), -weights * jnp.sin(angles)], 0)


def cross_spectra(left_rows, right_rows):
    half = left_rows.shape[-1] // 2
    left_real = left_rows[..., :half].astype(jnp.float32)[..., :, None, :]
    left_imag = left_rows[..., half:].astype(jnp.float32)[..., :, None, :]
    right_real = right_rows[..., :half].astype(jnp.float32)[..., None, :, :]
    right_imag = right_rows[..., half:].astype(jnp.float32)[..., None, :, :]
    real_part = left_real * right_real + left_imag * right_imag
    imag_part = left_imag * right_real - left_real * right_imag
    return jnp.concatenate([real_part, imag_part], -1)


def body(spectra, band_gain):
    lag_table = make_table(band_gain)
    group_rows = spectra.shape[1]
    all_channels = group_rows * lax.axis_size("chan")
    initial = jnp.zeros((spectra.shape[1], lag_table.shape[1], all_channels), jnp.float32)
    partner = lax.all_gather(spectra, "chan", axis=1, tiled=True)
    count_rows = partner.shape[1]
    block_rows = math.gcd(count_rows, 32)

    def one_block(block_index, running):
        partner_block = lax.dynamic_slice_in_dim(partner, block_index * block_rows, block_rows, 1)
        products = cross_spectra(spectra, partner_block)
        result = jnp.einsum("sijf,fl->ilj", products, lag_table, precision=lax.Precision.HIGHEST)
        column = block_index * block_rows
        return lax.dynamic_update_slice(running, result, (0, 0, column))

    stack_sum = lax.fori_loop(0, count_rows // block_rows, one_block, initial)
    return lax.psum_scatter(stack_sum, "seg", scatter_dimension=0, tiled=True)


def solution(mesh):
    return jax.shard_map(
        body,
        mesh=mesh,
        in_specs=(P("seg", "chan", None), P()),
        out_specs=P(("chan", "seg"), None, None),
        check_vma=False,
    )
```

profile of v0, /device:TPU:1, one launch (start us, length us, event | category | flops | bytes accessed | tf_op | source)
XLA Modules:
  0.0 225.8 jit_solution(7013793248653819583)
XLA Ops:
  6.5 1.4 copy.4
  8.1 0.7 broadcast_multiply_fusion
  8.8 6.8 %cosine_multiply_fusion = (f32[2048,201]{0,1:T(8,128)S(1)}, f32[2048,201]{0,1:T(8,128)S(1)}) fusion(s32[201]{0:T(256)S(1)} %iota_add_fusion, f32[2048]{0:T(1024)S(1)} %get-tuple-element.121, f32[2048]{0:T(1024)S(1)} %get-tuple-element.122), kind=kLoop, calls=%fused_computation.24 | loop fusion | flops 6586368 | bytes 3310372 | tf_op jit(solution)/shard_map/mul | solution.py:18
  15.6 0.3 pad_maximum_fusion
  16.0 123.5 %all-gather.2.cloned.1.call-done = bf16[1,256,4096]{2,0,1:T(2,128)(2,1)} async-done(((bf16[1,4,4096]{2,0,1:T(2,128)(2,1)}), bf16[1,256,4096]{2,0,1:T(2,128)(2,1)}) %all-gather.2.cloned.1.call-update) | async-done | bytes 2097168 | tf_op jit(solution)/shard_map/all_gather | solution.py:37
  139.4 5.8 %copy.5 = bf16[1,256,4096]{2,1,0:T(8,128)(2,1)} copy(bf16[1,256,4096]{2,0,1:T(2,128)(2,1)} %all-gather.2.cloned.1.call-done) | data formatting | bytes 4194304 | tf_op jit(solution)/shard_map/while | solution.py:48
  145.3 1.1 broadcast_in_dim.18
  146.3 45.5 %while.13 = (s32[]{:T(128)}, f32[4,201,256]{1,2,0:T(8,128)}, bf16[1,4,4096]{2,1,0:T(4,128)(2,1)S(1)}, bf16[1,256,4096]{2,1,0:T(8,128)(2,1)}, f32[4096,201]{0,1:T...) while((s32[]{:T(128)}, f32[4,201,256]{1,2,0:T(8,128)}, ...), condition=%wide.region_1.2_spmd, body=%wide.region_0.1_spmd.sunk | while | flops 1266827264 | bytes 9093291 | solution.py:48
  146.3 1.0 fusion.24
  147.4 0.3 multiply_add_fusion.2
  147.7 4.4 %fusion.25 = f32[4,201,256]{1,2,0:T(8,128)} fusion(f32[4,201,256]{1,2,0:T(8,128)} %get-tuple-element.179, s32[]{:T(128)S(6)} %select_n.28, f32[4096,201]{0,1:T(8,128)S(1)} %get-tuple-element.192, f32[1,4,32,2048]{3,2,1,0:T(8,128)S(1)} %get-tuple-element.166, f32[1,4,32,2048]{3,2,1,0:T(8,128)S(1)} %get-tuple-element.167), kind=kOutput, calls=%fused_computation.6.clone.1 | convolution fusion | flops 1265106944 | bytes 5521412 | tf_op jit(solution)/shard_map/while/body/eval_jaxpr/sijf,fl->ilj/dot_general | solution.py:44
  152.0 1.0 fusion.24
  153.1 0.3 multiply_add_fusion.2
  153.4 4.4 %fusion.25 = f32[4,201,256]{1,2,0:T(8,128)} fusion(f32[4,201,256]{1,2,0:T(8,128)} %get-tuple-element.179, s32[]{:T(128)S(6)} %select_n.28, f32[4096,201]{0,1:T(8,128)S(1)} %get-tuple-element.192, f32[1,4,32,2048]{3,2,1,0:T(8,128)S(1)} %get-tuple-element.166, f32[1,4,32,2048]{3,2,1,0:T(8,128)S(1)} %get-tuple-element.167), kind=kOutput, calls=%fused_computation.6.clone.1 | convolution fusion | flops 1265106944 | bytes 5521412 | tf_op jit(solution)/shard_map/while/body/eval_jaxpr/sijf,fl->ilj/dot_general | solution.py:44
  157.7 1.0 fusion.24
  158.8 0.3 multiply_add_fusion.2
  159.1 4.4 %fusion.25 = f32[4,201,256]{1,2,0:T(8,128)} fusion(f32[4,201,256]{1,2,0:T(8,128)} %get-tuple-element.179, s32[]{:T(128)S(6)} %select_n.28, f32[4096,201]{0,1:T(8,128)S(1)} %get-tuple-element.192, f32[1,4,32,2048]{3,2,1,0:T(8,128)S(1)} %get-tuple-element.166, f32[1,4,32,2048]{3,2,1,0:T(8,128)S(1)} %get-tuple-element.167), kind=kOutput, calls=%fused_computation.6.clone.1 | convolution fusion | flops 1265106944 | bytes 5521412 | tf_op jit(solution)/shard_map/while/body/eval_jaxpr/sijf,fl->ilj/dot_general | solution.py:44
  163.4 1.0 fusion.24
  164.7 4.4 %fusion.25 = f32[4,201,256]{1,2,0:T(8,128)} fusion(f32[4,201,256]{1,2,0:T(8,128)} %get-tuple-element.179, s32[]{:T(128)S(6)} %select_n.28, f32[4096,201]{0,1:T(8,128)S(1)} %get-tuple-element.192, f32[1,4,32,2048]{3,2,1,0:T(8,128)S(1)} %get-tuple-element.166, f32[1,4,32,2048]{3,2,1,0:T(8,128)S(1)} %get-tuple-element.167), kind=kOutput, calls=%fused_computation.6.clone.1 | convolution fusion | flops 1265106944 | bytes 5521412 | tf_op jit(solution)/shard_map/while/body/eval_jaxpr/sijf,fl->ilj/dot_general | solution.py:44
  169.1 1.0 fusion.24
  170.4 4.4 %fusion.25 = f32[4,201,256]{1,2,0:T(8,128)} fusion(f32[4,201,256]{1,2,0:T(8,128)} %get-tuple-element.179, s32[]{:T(128)S(6)} %select_n.28, f32[4096,201]{0,1:T(8,128)S(1)} %get-tuple-element.192, f32[1,4,32,2048]{3,2,1,0:T(8,128)S(1)} %get-tuple-element.166, f32[1,4,32,2048]{3,2,1,0:T(8,128)S(1)} %get-tuple-element.167), kind=kOutput, calls=%fused_computation.6.clone.1 | convolution fusion | flops 1265106944 | bytes 5521412 | tf_op jit(solution)/shard_map/while/body/eval_jaxpr/sijf,fl->ilj/dot_general | solution.py:44
  174.8 1.0 fusion.24
  176.1 4.4 %fusion.25 = f32[4,201,256]{1,2,0:T(8,128)} fusion(f32[4,201,256]{1,2,0:T(8,128)} %get-tuple-element.179, s32[]{:T(128)S(6)} %select_n.28, f32[4096,201]{0,1:T(8,128)S(1)} %get-tuple-element.192, f32[1,4,32,2048]{3,2,1,0:T(8,128)S(1)} %get-tuple-element.166, f32[1,4,32,2048]{3,2,1,0:T(8,128)S(1)} %get-tuple-element.167), kind=kOutput, calls=%fused_computation.6.clone.1 | convolution fusion | flops 1265106944 | bytes 5521412 | tf_op jit(solution)/shard_map/while/body/eval_jaxpr/sijf,fl->ilj/dot_general | solution.py:44
  180.5 1.0 fusion.24
  181.5 0.3 multiply_add_fusion.2
  181.8 4.4 %fusion.25 = f32[4,201,256]{1,2,0:T(8,128)} fusion(f32[4,201,256]{1,2,0:T(8,128)} %get-tuple-element.179, s32[]{:T(128)S(6)} %select_n.28, f32[4096,201]{0,1:T(8,128)S(1)} %get-tuple-element.192, f32[1,4,32,2048]{3,2,1,0:T(8,128)S(1)} %get-tuple-element.166, f32[1,4,32,2048]{3,2,1,0:T(8,128)S(1)} %get-tuple-element.167), kind=kOutput, calls=%fused_computation.6.clone.1 | convolution fusion | flops 1265106944 | bytes 5521412 | tf_op jit(solution)/shard_map/while/body/eval_jaxpr/sijf,fl->ilj/dot_general | solution.py:44
  186.2 1.0 fusion.24
  187.2 0.3 multiply_add_fusion.2
  187.5 4.4 %fusion.25 = f32[4,201,256]{1,2,0:T(8,128)} fusion(f32[4,201,256]{1,2,0:T(8,128)} %get-tuple-element.179, s32[]{:T(128)S(6)} %select_n.28, f32[4096,201]{0,1:T(8,128)S(1)} %get-tuple-element.192, f32[1,4,32,2048]{3,2,1,0:T(8,128)S(1)} %get-tuple-element.166, f32[1,4,32,2048]{3,2,1,0:T(8,128)S(1)} %get-tuple-element.167), kind=kOutput, calls=%fused_computation.6.clone.1 | convolution fusion | flops 1265106944 | bytes 5521412 | tf_op jit(solution)/shard_map/while/body/eval_jaxpr/sijf,fl->ilj/dot_general | solution.py:44
  191.9 2.5 %copy.6 = f32[4,201,256]{2,1,0:T(8,128)} copy(f32[4,201,256]{1,2,0:T(8,128)} %get-tuple-element.99) | data formatting | bytes 1646592 | tf_op jit(solution)/shard_map/while | solution.py:48
  194.4 22.7 %reduce-scatter.2.cloned.1.call-done = f32[1,201,256]{2,1,0:T(8,128)} async-done(((f32[4,201,256]{2,1,0:T(8,128)}), f32[1,201,256]{2,1,0:T(8,128)}) %reduce-scatter.2.cloned.1.call-update) | async-done | bytes 205840 | tf_op jit(solution)/shard_map/reduce_scatter | solution.py:49
  217.1 1.8 copy.7
  (18 shorter events, 1.0 us)
Async XLA Ops:
  6.5 132.9 %all-gather.2.cloned.1.call-start = ((), (), s32[]{:S(2)}) async-start(), calls=%async_computation.1 | async-start | bytes 4259840 | tf_op jit(solution)/shard_map/all_gather | solution.py:37
  8.0 209.1 %reduce-scatter.2.cloned.1.call-start = ((), (), s32[]{:S(2)}) async-start(), calls=%async_computation.2 | async-start | bytes 1064960 | tf_op jit(solution)/shard_map/reduce_scatter | solution.py:49
  15.9 130.4 %copy-start = (bf16[1,4,4096]{2,1,0:T(4,128)(2,1)S(1)}, bf16[1,4,4096]{2,1,0:T(4,128)(2,1)}, u32[]{:S(2)}) copy-start(bf16[1,4,4096]{2,1,0:T(4,128)(2,1)} %param.4) | copy-start | bytes 98308
Sparse Core Ops, SparseCore 0:
  10.9 128.5 all-gather.1
  194.6 22.5 reduce-scatter.1
where the time goes:
time: 226 us
  waiting for transfers between devices  146 us (65%)
  matrix products  35 us (15%)
  other arithmetic  18.2 us (8%)
  between operations  13.4 us (6%)
  local copies, waits for them, and re-layouts  12.7 us (6%)
    all_gather x1, waiting for transfers between devices, body(): partner = lax.all_gather(spectra, 'chan', axis=1, tiled=True)  123 us
    dot_general x8, matrix products, one_block(): jnp.einsum('sijf,fl->ilj', products, lag_table, precision=lax.Precision.H...  35 us
    reduce_scatter x1, waiting for transfers between devices, body(): return lax.psum_scatter(stack_sum, 'seg', scatter_dimension=0, tiled=True)  22.7 us
    while x2, local copies, waits for them, and re-layouts, body(): stack_sum = lax.fori_loop(0, count_rows // block_rows, one_block, initial)  8.38 us
    mul x16, other arithmetic, cross_spectra(): real_part = left_real * right_real + left_imag * right_imag  8.08 us
    mul x1, other arithmetic, make_table(): weights * jnp.cos(angles)  6.83 us
  transfers between devices with their start and end apart: 2, of which 2 were waited for; matrix products, arithmetic and copies ran while one was open for 3% of the time, Pallas kernels for 0%

commit v1 on v0

v1 whole, which is shorter than its diff:
```python
import functools
import math

import jax
import jax.numpy as jnp
from jax import lax
from jax.experimental import pallas as pl
from jax.experimental.pallas import tpu as pltpu
from jax.sharding import PartitionSpec as P

MAXLAG = 100
MESH = pl.DeviceIdType.MESH


def place():
    c, s = lax.axis_index("chan"), lax.axis_index("seg")
    return (lax.rem(c // 8, 2) * 2 + s // 2, c // 16, lax.rem(c, 8), lax.rem(s, 2))


def device(x, y, z, core):
    return (y * 16 + (x // 2) * 8 + z, lax.rem(x, 2) * 2 + core)


def split(value):
    high = value.astype(jnp.bfloat16)
    return high, (value - high.astype(jnp.float32)).astype(jnp.bfloat16)


def kernel(x_ref, g_ref, out_ref, own, ibuf, jbuf, ifull, jfull, zh, zl, th, tl, base, steps,
           obuf, rbuf, own_sem, isend, irecv, jsend, jrecv, ksend, osend, orecv):
    x, y, z, k = place()
    xh, xl = x // 2, lax.rem(x, 2)
    half = g_ref.shape[1]
    tiles = half // 128

    barrier = pltpu.get_barrier_semaphore()
    load = pltpu.make_async_copy(x_ref.at[0], own, own_sem)
    load.start()

    def tell(target, me_too):
        @pl.when(jnp.logical_not(me_too))
        def _():
            pl.semaphore_signal(barrier, inc=1, device_id=target, device_id_type=MESH)

    @pl.loop(0, 16)
    def _(n):
        sy, ss = n // 4, lax.rem(n, 4)
        sx, sk = k * 2 + ss // 2, lax.rem(ss, 2)
        tell(device(sx, sy, z, sk), (sx == x) & (sy == y) & (sk == k))

    @pl.loop(0, 8)
    def _(n):
        sz, sx = (n // 2) * 2 + xl, xh * 2 + lax.rem(n, 2)
        tell(device(sx, y, sz, k), (sx == x) & (sz == z))

    tell(device(x, y, z, 1 - k), False)

    i_self = (k == xh).astype(jnp.int32)
    j_self = (lax.rem(z, 2) == xl).astype(jnp.int32)
    load.wait()
    pl.semaphore_wait(barrier, 25 - i_self - j_self)

    my_i_slot = y * 4 + xl * 2 + k
    my_j_slot = (z // 2) * 4 + xl * 2 + k

    def i_copy(n):
        tx, ty = lax.rem(x + n // 4, 4), lax.rem(y + n, 4)
        there = device(tx, ty, z, xh)
        return pltpu.make_async_remote_copy(own, ibuf.at[my_i_slot], isend.at[n], irecv.at[my_i_slot],
                                            device_id=there, device_id_type=MESH)

    def j_copy(n):
        tx, tz = xh * 2 + lax.rem(z, 2), lax.rem(z + n, 8)
        there = device(tx, y, tz, k)
        return pltpu.make_async_remote_copy(own, jbuf.at[my_j_slot], jsend.at[n], jrecv.at[my_j_slot],
                                            device_id=there, device_id_type=MESH)

    i_mine = pltpu.make_async_copy(own, ibuf.at[my_i_slot], irecv.at[my_i_slot])
    j_mine = pltpu.make_async_copy(own, jbuf.at[my_j_slot], jrecv.at[my_j_slot])

    @pl.loop(1, 8)
    def _(n):
        j_copy(n).start()

    @pl.loop(1, 16)
    def _(n):
        i_copy(n).start()

    @pl.when(j_self == 1)
    def _():
        j_mine.start()

    @pl.when(j_self == 0)
    def _():
        j_copy(0).start()

    @pl.when(i_self == 1)
    def _():
        i_mine.start()

    @pl.when(i_self == 0)
    def _():
        i_copy(0).start()

    def phases(first, step, rows):
        f = lax.broadcasted_iota(jnp.int32, (rows, 256), 0) * step + first
        lag = lax.broadcasted_iota(jnp.int32, (rows, 256), 1) - MAXLAG
        turn = jnp.bitwise_and(f * lag + half, 2 * half - 1) - half
        return turn.astype(jnp.float32) * (math.pi / half)

    angle = phases(0, 1, 128)
    base[0] = jnp.cos(angle)
    base[1] = jnp.sin(angle)
    angle = phases(0, 128, tiles)
    steps[0] = jnp.cos(angle)
    steps[1] = jnp.sin(angle)

    @pl.loop(0, tiles)
    def _(t):
        c, s = steps[0, pl.ds(t, 1), :], steps[1, pl.ds(t, 1), :]
        high, low = split(base[0] * c - base[1] * s)
        th[t, 0:128], tl[t, 0:128] = high, low
        high, low = split(base[1] * c + base[0] * s)
        th[t, 128:256], tl[t, 128:256] = high, low

    def relay(n):
        slot = n * 2 + k
        return pltpu.make_async_remote_copy(jbuf.at[slot], jbuf.at[slot], ksend.at[n], jrecv.at[slot],
                                            device_id=device(x, y, z, 1 - k), device_id_type=MESH)

    def landed(buf, sem, slot):
        pltpu.make_async_copy(buf.at[slot], buf.at[slot], sem.at[slot]).wait()

    @pl.loop(0, 8)
    def _(n):
        landed(jbuf, jrecv, n * 2 + k)
        relay(n).start()

    gain = g_ref[...] * (1.0 / math.sqrt(half))

    @pl.loop(0, 16)
    def _(n):
        landed(ibuf, irecv, n)
        ifull[n, :, 0:half] = ibuf[n, :, 0:half].astype(jnp.float32) * gain
        ifull[n, :, half:] = ibuf[n, :, half:].astype(jnp.float32) * gain

    @pl.loop(0, 8)
    def _(n):
        landed(jbuf, jrecv, n * 2 + 1 - k)

    @pl.loop(0, 4)
    def _(s):
        for p in range(2):
            jfull[s, p] = jnp.concatenate(
                [jbuf[8 * p + s].astype(jnp.float32), jbuf[8 * p + 4 + s].astype(jnp.float32)], 0)

    @pl.loop(0, tiles)
    def _(t):
        re = pl.ds(pl.multiple_of(t * 128, 128), 128)
        im = pl.ds(pl.multiple_of(half + t * 128, 128), 128)
        jr = [[jfull[s, p, :, re] for p in range(2)] for s in range(4)]
        ji = [[jfull[s, p, :, im] for p in range(2)] for s in range(4)]
        for i in range(16):
            ir = [ifull[(i // 4) * 4 + s, i % 4:i % 4 + 1, re] for s in range(4)]
            ii = [ifull[(i // 4) * 4 + s, i % 4:i % 4 + 1, im] for s in range(4)]
            zr, zi = [], []
            for p in range(2):
                zr.append(sum(ir[s] * jr[s][p] + ii[s] * ji[s][p] for s in range(4)))
                zi.append(sum(ir[s] * ji[s][p] - ii[s] * jr[s][p] for s in range(4)))
            high, low = split(jnp.concatenate(zr, 0))
            zh[t, i * 16:i * 16 + 16, 0:128], zl[t, i * 16:i * 16 + 16, 0:128] = high, low
            high, low = split(jnp.concatenate(zi, 0))
            zh[t, i * 16:i * 16 + 16, 128:256], zl[t, i * 16:i * 16 + 16, 128:256] = high, low

    obuf[...] = jnp.zeros_like(obuf)

    @pl.loop(0, tiles)
    def _(t):
        dot = functools.partial(jnp.dot, preferred_element_type=jnp.float32)
        obuf[...] += dot(zh[t], th[t]) + dot(zl[t], th[t]) + dot(zh[t], tl[t])

    my_o_slot = y * 4 + x

    def o_copy(i):
        there = device(k * 2 + lax.rem(i, 4) // 2, i // 4, z, lax.rem(i, 2))
        return pltpu.make_async_remote_copy(obuf.at[pl.ds(pl.multiple_of(i * 16, 16), 16)], rbuf.at[my_o_slot], osend.at[i],
                                            orecv.at[my_o_slot], device_id=there, device_id_type=MESH)

    own_row = my_i_slot

    @pl.loop(0, 16)
    def _(i):
        mine = (i_self == 1) & (i == own_row)

        @pl.when(mine)
        def _():
            pltpu.make_async_copy(obuf.at[pl.ds(pl.multiple_of(i * 16, 16), 16)], rbuf.at[my_o_slot], orecv.at[my_o_slot]).start()

        @pl.when(jnp.logical_not(mine))
        def _():
            o_copy(i).start()

    @pl.loop(0, 16)
    def _(n):
        landed(rbuf, orecv, n)

    for b in range(8):
        rows = []
        for m in range(4):
            rows += [rbuf[2 * b, 4 * m:4 * m + 4, :], rbuf[2 * b + 1, 4 * m:4 * m + 4, :]]
        joined = jnp.concatenate(rows, 0)
        base[b // 4, (b % 4) * 32:(b % 4) * 32 + 32, :] = joined

    for h in range(2):
        out_ref[0, :, h * 128:(h + 1) * 128] = base[h].T[0:2 * MAXLAG + 1]

    @pl.loop(1, 8)
    def _(n):
        j_copy(n).wait_send()

    @pl.loop(1, 16)
    def _(n):
        i_copy(n).wait_send()

    @pl.when(j_self == 0)
    def _():
        j_copy(0).wait_send()

    @pl.when(i_self == 0)
    def _():
        i_copy(0).wait_send()

    @pl.loop(0, 8)
    def _(n):
        relay(n).wait_send()

    @pl.loop(0, 16)
    def _(i):
        @pl.when(jnp.logical_not((i_self == 1) & (i == own_row)))
        def _():
            o_copy(i).wait_send()


def body(spectra, band_gain):
    half = band_gain.shape[0]
    tiles = half // 128
    f32, b16 = jnp.float32, jnp.bfloat16
    dma = pltpu.SemaphoreType.DMA
    return pl.pallas_call(
        kernel,
        out_shape=jax.ShapeDtypeStruct((1, 2 * MAXLAG + 1, 256), f32),
        in_specs=[pl.BlockSpec(memory_space=pl.ANY), pl.BlockSpec(memory_space=pltpu.VMEM)],
        out_specs=pl.BlockSpec(memory_space=pltpu.VMEM),
        scratch_shapes=[
            pltpu.VMEM((4, 2 * half), b16),
            pltpu.VMEM((16, 4, 2 * half), b16),
            pltpu.VMEM((16, 4, 2 * half), b16),
            pltpu.VMEM((16, 4, 2 * half), f32),
            pltpu.VMEM((4, 2, 8, 2 * half), f32),
            pltpu.VMEM((tiles, 256, 256), b16),
            pltpu.VMEM((tiles, 256, 256), b16),
            pltpu.VMEM((tiles, 256, 256), b16),
            pltpu.VMEM((tiles, 256, 256), b16),
            pltpu.VMEM((2, 128, 256), f32),
            pltpu.VMEM((2, tiles, 256), f32),
            pltpu.VMEM((256, 256), f32),
            pltpu.VMEM((16, 16, 256), f32),
            dma, dma((16,)), dma((16,)), dma((8,)), dma((16,)), dma((8,)), dma((16,)), dma((16,)),
        ],
        compiler_params=pltpu.CompilerParams(
            collective_id=0, has_side_effects=True, vmem_limit_bytes=48 * 2**20),
        name="correlate",
    )(spectra, band_gain.reshape(1, half))


def solution(mesh):
    return jax.shard_map(
        body,
        mesh=mesh,
        in_specs=(P("seg", "chan", None), P()),
        out_specs=P(("chan", "seg"), None, None),
        check_vma=False,
    )
```

time: 226 us -> 38.2 us (0.17)
  waiting for transfers between devices: 146 us -> 0 us
  Pallas kernels: 0 us -> 35.6 us
  matrix products: 35 us -> 0 us
  other arithmetic: 18.2 us -> 0 us
  between operations: 13.4 us -> 0.01 us
  local copies, waits for them, and re-layouts: 12.7 us -> 2.35 us
    all_gather x1 -> x0, waiting for transfers between devices: 123 us -> none  [body(): partner = lax.all_gather(spectra, 'chan', axis=1, tiled=True)]
    pallas_call x0 -> x1, Pallas kernels: none -> 35.6 us  [body(): pl.pallas_call(kernel, out_shape=jax.ShapeDtypeStruct((1, 2 * MAXLAG + 1,...]
    dot_general x8 -> x0, matrix products: 35 us -> none  [one_block(): jnp.einsum('sijf,fl->ilj', products, lag_table, precision=lax.Precision.H...]
    reduce_scatter x1 -> x0, waiting for transfers between devices: 22.7 us -> none  [body(): return lax.psum_scatter(stack_sum, 'seg', scatter_dimension=0, tiled=True)]
    mul x17 -> x0, other arithmetic: 14.9 us -> none  [the longest x16 8.08 us: cross_spectra(): real_part = left_real * right_real + left_imag * right_imag]
    while x2 -> x0, local copies, waits for them, and re-layouts: 8.38 us -> none  [body(): stack_sum = lax.fori_loop(0, count_rows // block_rows, one_block, initial)]
    add x8 -> x0, other arithmetic: 2.28 us -> none  [cross_spectra(): real_part = left_real * right_real + left_imag * right_imag]
  transfers between devices with their start and end apart: 2 -> 0, of which waited for: 2 -> 0; matrix products, arithmetic and copies ran while one was open for 3% -> 0% of each run, Pallas kernels for 0% -> 0%
where the time goes in v1:
time: 38.2 us; the launch traced here: 38 us
  Pallas kernels  35.6 us (93%)
  local copies, waits for them, and re-layouts  2.35 us (6%)
    pallas_call x1, Pallas kernels, body(): pl.pallas_call(kernel, out_shape=jax.ShapeDtypeStruct((1, 2 * MAXLAG + 1,...  35.6 us
    unnamed x4, local copies, waits for them, and re-layouts  1.45 us
    pallas_call x1, local copies, waits for them, and re-layouts, body(): pl.pallas_call(kernel, out_shape=jax.ShapeDtypeStruct((1, 2 * MAXLAG + 1,...  0.89 us

profile of v1, /device:TPU:1, one launch (start us, length us, event | category | flops | bytes accessed | tf_op | source)
XLA Modules:
  0.0 38.0 jit_solution(10033878841611625108)
XLA Ops:
  0.0 0.0 copy-start
  0.0 0.8 %copy-done = bf16[1,4,4096]{2,1,0:T(4,128)(2,1)S(1)} copy-done((bf16[1,4,4096]{2,1,0:T(4,128)(2,1)S(1)}, bf16[1,4,4096]{2,1,0:T(4,128)(2,1)}, u32[]{:S(2)}) %copy-start) | copy-done | bytes 32792
  0.8 0.0 copy-start.1
  0.8 0.7 %copy-done.1 = f32[2048]{0:T(1024)S(1)} copy-done((f32[2048]{0:T(1024)S(1)}, f32[2048]{0:T(1024)}, u32[]{:S(2)}) %copy-start.1) | copy-done | bytes 8216
  1.5 35.6 %correlate.1 = f32[1,201,256]{2,1,0:T(8,128)S(1)} custom-call(bf16[1,4,4096]{2,1,0:T(4,128)(2,1)S(1)} %copy-done, f32[1,2048]{1,0:T(1,128)S(1)} %bitcast.1), custom_call_target="tpu_custom_call" | custom-call | tf_op jit(solution)/shard_map/correlate/pallas_call | solution.py:249
  37.1 0.9 %copy.3 = f32[1,201,256]{2,0,1:T(1,128)} copy(f32[1,201,256]{2,1,0:T(8,128)S(1)} %correlate.1) | data formatting | bytes 411648 | tf_op jit(solution)/shard_map/correlate/pallas_call | solution.py:249
Async XLA Ops:
  0.0 0.8 %copy-start = (bf16[1,4,4096]{2,1,0:T(4,128)(2,1)S(1)}, bf16[1,4,4096]{2,1,0:T(4,128)(2,1)}, u32[]{:S(2)}) copy-start(bf16[1,4,4096]{2,1,0:T(4,128)(2,1)} %x_ref.1) | copy-start | bytes 98308
  0.8 0.7 %copy-start.1 = (f32[2048]{0:T(1024)S(1)}, f32[2048]{0:T(1024)}, u32[]{:S(2)}) copy-start(f32[2048]{0:T(1024)} %param.3) | copy-start | bytes 24580

commit v2 on v0

v2 whole, which is shorter than its diff:
```python
import functools
import math

import jax
import jax.numpy as jnp
from jax import lax
from jax.experimental import pallas as pl
from jax.experimental.pallas import tpu as pltpu
from jax.sharding import PartitionSpec as P

MAXLAG = 100
MESH = pl.DeviceIdType.MESH
BEHIND = [2, 3, 1, 0]
STAGED = False


def place():
    c, s = lax.axis_index("chan"), lax.axis_index("seg")
    return (lax.rem(c // 8, 2) * 2 + s // 2, c // 16, lax.rem(c, 8), lax.rem(s, 2))


def device(x, y, z, core):
    return (y * 16 + (x // 2) * 8 + z, lax.rem(x, 2) * 2 + core)


def split(value):
    high = value.astype(jnp.bfloat16)
    return high, (value - high.astype(jnp.float32)).astype(jnp.bfloat16)


def added(terms):
    return (terms[0] + terms[1]) + (terms[2] + terms[3])


def either(condition, yes, no):
    pl.when(condition)(yes)
    pl.when(jnp.logical_not(condition))(no)


def kernel(x_ref, g_ref, out_ref, own, gains, ibuf, jbuf, ifull, jfull, zh, zl, th, tl, base, steps,
           obuf, rbuf, own_sem, gain_sem, isend, irecv, jsend, jrecv, ksend, krecv, osend, orecv):
    x, y, z, k = place()
    xh, xl = x // 2, lax.rem(x, 2)
    half = x_ref.shape[2] // 2
    tiles = half // 128
    group = z // 4

    barrier = pltpu.get_barrier_semaphore()

    def signal(target):
        pl.semaphore_signal(barrier, inc=1, device_id=target, device_id_type=MESH)

    load = pltpu.make_async_copy(x_ref.at[0], own, own_sem)
    load.start()
    load_gain = pltpu.make_async_copy(g_ref, gains, gain_sem)
    load_gain.start()

    @pl.loop(0, 8)
    def _(n):
        sx, sz = xh * 2 + lax.rem(n, 2), (n // 2) * 2 + xl
        pl.when(jnp.logical_not((sx == x) & (sz == z)))(lambda: signal(device(sx, y, sz, k)))

    @pl.loop(0, 16)
    def _(n):
        sy, ss = n // 4, lax.rem(n, 4)
        sx, sk = k * 2 + ss // 2, lax.rem(ss, 2)
        pl.when(jnp.logical_not((sx == x) & (sy == y) & (sk == k)))(lambda: signal(device(sx, sy, z, sk)))

    signal(device(x, y, z, 1 - k))

    def phases(first, step, rows):
        f = lax.broadcasted_iota(jnp.int32, (rows, 256), 0) * step + first
        lag = lax.broadcasted_iota(jnp.int32, (rows, 256), 1) - MAXLAG
        turn = jnp.bitwise_and(f * lag + half, 2 * half - 1) - half
        return turn.astype(jnp.float32) * (math.pi / half)

    angle = phases(0, 1, 128)
    base[0] = jnp.cos(angle)
    base[1] = jnp.sin(angle)
    angle = phases(0, 128, tiles)
    steps[0] = jnp.cos(angle)
    steps[1] = jnp.sin(angle)

    i_self = k == xh
    j_self = lax.rem(z, 2) == xl
    load.wait()
    load_gain.wait()
    pl.semaphore_wait(barrier, 25 - i_self.astype(jnp.int32) - j_self.astype(jnp.int32))

    my_seg = xl * 2 + k
    my_j = lax.rem(z // 2, 2) * 2 + xl

    def ring_sends(g):
        @pl.loop(0, 4)
        def _(n):
            tz = g * 4 + lax.rem(z + 2 + n, 4)
            either(j_self & (tz == z),
                   lambda: pltpu.make_async_copy(own, jbuf.at[k, group, my_j], jrecv.at[group]).start(),
                   lambda: pltpu.make_async_remote_copy(
                       own, jbuf.at[k, group, my_j], jsend.at[g], jrecv.at[group],
                       device_id=device(xh * 2 + lax.rem(z, 2), y, tz, k), device_id_type=MESH).start())

    def plane_send(dx, dy):
        spot = BEHIND.index((4 - dy) % 4)
        pltpu.make_async_remote_copy(own, ibuf.at[spot * 4 + my_seg], isend, irecv.at[spot // 2],
                                     device_id=device(lax.rem(x + dx, 4), lax.rem(y + dy, 4), z, xh), device_id_type=MESH).start()

    def left(ref, sem):
        return lambda: pltpu.make_async_copy(ref, ref, sem).wait()

    def ring_left(g):
        either(j_self & (group == g), left(ibuf.at[pl.ds(0, 3)], jsend.at[g]), left(ibuf.at[pl.ds(0, 4)], jsend.at[g]))

    ring_sends(0)
    for spot in range(4):
        dy = (4 - BEHIND[spot]) % 4
        for dx in (2, 1, 3):
            plane_send(dx, dy)
        if dy:
            plane_send(0, dy)
        else:
            either(i_self, lambda: pltpu.make_async_copy(own, ibuf.at[12 + my_seg], irecv.at[1]).start(), lambda: plane_send(0, 0))
    if not STAGED:
        ring_sends(1)

    @pl.loop(0, tiles)
    def _(t):
        c, s = steps[0, pl.ds(t, 1), :], steps[1, pl.ds(t, 1), :]
        th[t, 0:128], tl[t, 0:128] = split(base[0] * c - base[1] * s)
        th[t, 128:256], tl[t, 128:256] = split(base[1] * c + base[0] * s)

    if STAGED:
        ring_left(0)
        ring_sends(1)

    def here(buf, sem):
        pltpu.make_async_copy(buf, buf, sem).wait()

    for turn in range(2):
        g = group if turn == 0 else 1 - group
        here(jbuf.at[k, g], jrecv.at[g])
        pltpu.make_async_remote_copy(jbuf.at[k, g], jbuf.at[k, g], ksend.at[g], krecv.at[g],
                                     device_id=device(x, y, z, 1 - k), device_id_type=MESH).start()

    dot = functools.partial(jnp.dot, preferred_element_type=jnp.float32)
    scale = 1.0 / math.sqrt(half)
    my_o = y * 4 + x

    for part in range(2):
        here(ibuf.at[pl.ds(8 * part, 8)], irecv.at[part])

        @pl.loop(0, 2)
        def _(n, part=part):
            for s in range(4):
                real = ibuf[8 * part + 4 * n + s, :, 0:half].astype(jnp.float32) * (gains[...] * scale)
                imag = ibuf[8 * part + 4 * n + s, :, half:].astype(jnp.float32) * (gains[...] * scale)
                ifull[n, s, :, 0:half] = real
                ifull[n, s, :, half:2 * half] = imag
                ifull[n, s, :, 2 * half:] = real + imag

        if part == 0:
            for g in range(2):
                here(jbuf.at[1 - k, g], krecv.at[g])
            for s in range(4):
                for g in range(2):
                    jfull[s, g] = jnp.concatenate([jbuf[s % 2, g, s // 2].astype(jnp.float32),
                                                   jbuf[s % 2, g, 2 + s // 2].astype(jnp.float32)], 0)

        @pl.loop(0, tiles)
        def _(t):
            re = pl.ds(pl.multiple_of(t * 128, 128), 128)
            im = pl.ds(pl.multiple_of(half + t * 128, 128), 128)
            both = pl.ds(pl.multiple_of(2 * half + t * 128, 128), 128)
            jr = [[jfull[s, g, :, re] for g in range(2)] for s in range(4)]
            ji = [[jfull[s, g, :, im] for g in range(2)] for s in range(4)]
            jd = [[jr[s][g] - ji[s][g] for g in range(2)] for s in range(4)]
            for i in range(8):
                ib = [ifull[i // 4, s, i % 4:i % 4 + 1, both] for s in range(4)]
                ir = [ifull[i // 4, s, i % 4:i % 4 + 1, re] for s in range(4)]
                ii = [ifull[i // 4, s, i % 4:i % 4 + 1, im] for s in range(4)]
                zr, zi = [], []
                for g in range(2):
                    rr = added([ir[s] * jr[s][g] for s in range(4)])
                    ss = added([ii[s] * ji[s][g] for s in range(4)])
                    bd = added([ib[s] * jd[s][g] for s in range(4)])
                    zr.append(rr + ss)
                    zi.append((rr - ss) - bd)
                rows = slice(i * 16, i * 16 + 16)
                zh[t, rows, 0:128], zl[t, rows, 0:128] = split(jnp.concatenate(zr, 0))
                zh[t, rows, 128:256], zl[t, rows, 128:256] = split(jnp.concatenate(zi, 0))

        total = None
        for t in range(tiles):
            term = dot(zh[t], th[t]) + dot(zl[t], th[t]) + dot(zh[t], tl[t])
            total = term if total is None else total + term
        obuf[part] = total

        for n in range(8):
            spot, r = 2 * part + n // 4, n % 4
            block = obuf.at[part, pl.ds(n * 16, 16)]

            def give(block=block, spot=spot, r=r):
                pltpu.make_async_remote_copy(
                    block, rbuf.at[my_o], osend, orecv,
                    device_id=device(k * 2 + r // 2, lax.rem(y + BEHIND[spot], 4), z, r % 2), device_id_type=MESH).start()

            if BEHIND[spot]:
                give()
            else:
                either(i_self & (my_seg == r), lambda block=block: pltpu.make_async_copy(block, rbuf.at[my_o], orecv).start(), give)

    either(i_self, left(rbuf.at[pl.ds(0, 15)], osend), left(rbuf, osend))
    either(i_self, left(ibuf.at[pl.ds(0, 15)], isend), left(ibuf, isend))

    for g in range(1 if STAGED else 0, 2):
        ring_left(g)
    for g in range(2):
        pltpu.make_async_copy(jbuf.at[0, g], jbuf.at[0, g], ksend.at[g]).wait()

    here(rbuf, orecv)
    for b in range(8):
        rows = []
        for m in range(4):
            rows += [rbuf[2 * b, 4 * m:4 * m + 4, :], rbuf[2 * b + 1, 4 * m:4 * m + 4, :]]
        base[b // 4, (b % 4) * 32:(b % 4) * 32 + 32, :] = jnp.concatenate(rows, 0)

    for h in range(2):
        out_ref[0, :, h * 128:(h + 1) * 128] = base[h].T[0:2 * MAXLAG + 1]


def body(spectra, band_gain):
    half = band_gain.shape[0]
    tiles = half // 128
    f32, b16 = jnp.float32, jnp.bfloat16
    dma = pltpu.SemaphoreType.DMA
    return pl.pallas_call(
        kernel,
        out_shape=jax.ShapeDtypeStruct((1, 2 * MAXLAG + 1, 256), f32),
        in_specs=[pl.BlockSpec(memory_space=pltpu.HBM), pl.BlockSpec(memory_space=pltpu.HBM)],
        out_specs=pl.BlockSpec(memory_space=pltpu.VMEM),
        scratch_shapes=[
            pltpu.VMEM((4, 2 * half), b16),
            pltpu.VMEM((1, half), f32),
            pltpu.VMEM((16, 4, 2 * half), b16),
            pltpu.VMEM((2, 2, 4, 4, 2 * half), b16),
            pltpu.VMEM((2, 4, 4, 3 * half), f32),
            pltpu.VMEM((4, 2, 8, 2 * half), f32),
            pltpu.VMEM((tiles, 128, 256), b16),
            pltpu.VMEM((tiles, 128, 256), b16),
            pltpu.VMEM((tiles, 256, 256), b16),
            pltpu.VMEM((tiles, 256, 256), b16),
            pltpu.VMEM((2, 128, 256), f32),
            pltpu.VMEM((2, tiles, 256), f32),
            pltpu.VMEM((2, 128, 256), f32),
            pltpu.VMEM((16, 16, 256), f32),
            dma, dma, dma, dma((2,)), dma((2,)), dma((2,)), dma((2,)), dma((2,)), dma, dma,
        ],
        compiler_params=pltpu.CompilerParams(
            collective_id=0, has_side_effects=True, vmem_limit_bytes=48 * 2**20),
        name="correlate",
    )(spectra, band_gain.reshape(1, half))


def solution(mesh):
    return jax.shard_map(
        body,
        mesh=mesh,
        in_specs=(P("seg", "chan", None), P()),
        out_specs=P(("chan", "seg"), None, None),
        check_vma=False,
    )
```

time: 226 us -> 33.2 us (0.15)
  waiting for transfers between devices: 146 us -> 0 us
  matrix products: 35 us -> 0 us
  Pallas kernels: 0 us -> 30.7 us
  other arithmetic: 18.2 us -> 0 us
  between operations: 13.4 us -> 0.01 us
  local copies, waits for them, and re-layouts: 12.7 us -> 2.35 us
    all_gather x1 -> x0, waiting for transfers between devices: 123 us -> none  [body(): partner = lax.all_gather(spectra, 'chan', axis=1, tiled=True)]
    dot_general x8 -> x0, matrix products: 35 us -> none  [one_block(): jnp.einsum('sijf,fl->ilj', products, lag_table, precision=lax.Precision.H...]
    pallas_call x0 -> x1, Pallas kernels: none -> 30.7 us  [body(): pl.pallas_call(kernel, out_shape=jax.ShapeDtypeStruct((1, 2 * MAXLAG + 1,...]
    reduce_scatter x1 -> x0, waiting for transfers between devices: 22.7 us -> none  [body(): return lax.psum_scatter(stack_sum, 'seg', scatter_dimension=0, tiled=True)]
    mul x17 -> x0, other arithmetic: 14.9 us -> none  [the longest x16 8.08 us: cross_spectra(): real_part = left_real * right_real + left_imag * right_imag]
    while x2 -> x0, local copies, waits for them, and re-layouts: 8.38 us -> none  [body(): stack_sum = lax.fori_loop(0, count_rows // block_rows, one_block, initial)]
    add x8 -> x0, other arithmetic: 2.28 us -> none  [cross_spectra(): real_part = left_real * right_real + left_imag * right_imag]
  transfers between devices with their start and end apart: 2 -> 0, of which waited for: 2 -> 0; matrix products, arithmetic and copies ran while one was open for 3% -> 0% of each run, Pallas kernels for 0% -> 0%
where the time goes in v2:
time: 33.2 us; the launch traced here: 33.1 us
  Pallas kernels  30.7 us (92%)
  local copies, waits for them, and re-layouts  2.35 us (7%)
    pallas_call x1, Pallas kernels, body(): pl.pallas_call(kernel, out_shape=jax.ShapeDtypeStruct((1, 2 * MAXLAG + 1,...  30.7 us
    unnamed x4, local copies, waits for them, and re-layouts  1.45 us
    pallas_call x1, local copies, waits for them, and re-layouts, body(): pl.pallas_call(kernel, out_shape=jax.ShapeDtypeStruct((1, 2 * MAXLAG + 1,...  0.89 us

profile of v2, /device:TPU:1, one launch (start us, length us, event | category | flops | bytes accessed | tf_op | source)
XLA Modules:
  0.0 33.1 jit_solution(4430677795837548045)
XLA Ops:
  0.0 0.0 copy-start
  0.0 0.8 %copy-done = bf16[1,4,4096]{2,1,0:T(4,128)(2,1)S(1)} copy-done((bf16[1,4,4096]{2,1,0:T(4,128)(2,1)S(1)}, bf16[1,4,4096]{2,1,0:T(4,128)(2,1)}, u32[]{:S(2)}) %copy-start) | copy-done | bytes 32792
  0.8 0.0 copy-start.1
  0.8 0.7 %copy-done.1 = f32[2048]{0:T(1024)S(1)} copy-done((f32[2048]{0:T(1024)S(1)}, f32[2048]{0:T(1024)}, u32[]{:S(2)}) %copy-start.1) | copy-done | bytes 8216
  1.5 30.7 %correlate.1 = f32[1,201,256]{2,1,0:T(8,128)S(1)} custom-call(bf16[1,4,4096]{2,1,0:T(4,128)(2,1)S(1)} %copy-done, f32[1,2048]{1,0:T(1,128)S(1)} %bitcast.1), custom_call_target="tpu_custom_call" | custom-call | tf_op jit(solution)/shard_map/correlate/pallas_call | solution.py:236
  32.2 0.9 %copy.3 = f32[1,201,256]{2,0,1:T(1,128)} copy(f32[1,201,256]{2,1,0:T(8,128)S(1)} %correlate.1) | data formatting | bytes 411648 | tf_op jit(solution)/shard_map/correlate/pallas_call | solution.py:236
Async XLA Ops:
  0.0 0.8 %copy-start = (bf16[1,4,4096]{2,1,0:T(4,128)(2,1)S(1)}, bf16[1,4,4096]{2,1,0:T(4,128)(2,1)}, u32[]{:S(2)}) copy-start(bf16[1,4,4096]{2,1,0:T(4,128)(2,1)} %x_ref.1) | copy-start | bytes 98308
  0.8 0.7 %copy-start.1 = (f32[2048]{0:T(1024)S(1)}, f32[2048]{0:T(1024)}, u32[]{:S(2)}) copy-start(f32[2048]{0:T(1024)} %param.3) | copy-start | bytes 24580

commit v3 on v2

--- a/solution.py
+++ b/solution.py
@@ -37,8 +37,8 @@
     pl.when(jnp.logical_not(condition))(no)
 
 
-def kernel(x_ref, g_ref, out_ref, own, gains, ibuf, jbuf, ifull, jfull, zh, zl, th, tl, base, steps,
-           obuf, rbuf, own_sem, gain_sem, isend, irecv, jsend, jrecv, ksend, krecv, osend, orecv):
+def kernel(x_ref, g_ref, rbuf, own, gains, ibuf, jbuf, ifull, jfull, zh, zl, th, tl, base, steps,
+           obuf, own_sem, gain_sem, isend, irecv, jsend, jrecv, ksend, krecv, osend, orecv):
     x, y, z, k = place()
     xh, xl = x // 2, lax.rem(x, 2)
     half = x_ref.shape[2] // 2
@@ -218,6 +218,9 @@
         pltpu.make_async_copy(jbuf.at[0, g], jbuf.at[0, g], ksend.at[g]).wait()
 
     here(rbuf, orecv)
+
+
+def assemble(rbuf, out_ref, base):
     for b in range(8):
         rows = []
         for m in range(4):
@@ -225,7 +228,7 @@
         base[b // 4, (b % 4) * 32:(b % 4) * 32 + 32, :] = jnp.concatenate(rows, 0)
 
     for h in range(2):
-        out_ref[0, :, h * 128:(h + 1) * 128] = base[h].T[0:2 * MAXLAG + 1]
+        out_ref[:, 0, h * 128:(h + 1) * 128] = base[h].T[0:2 * MAXLAG + 1]
 
 
 def body(spectra, band_gain):
@@ -233,11 +236,11 @@
     tiles = half // 128
     f32, b16 = jnp.float32, jnp.bfloat16
     dma = pltpu.SemaphoreType.DMA
-    return pl.pallas_call(
+    blocks = pl.pallas_call(
         kernel,
-        out_shape=jax.ShapeDtypeStruct((1, 2 * MAXLAG + 1, 256), f32),
+        out_shape=jax.ShapeDtypeStruct((16, 16, 256), f32),
         in_specs=[pl.BlockSpec(memory_space=pltpu.HBM), pl.BlockSpec(memory_space=pltpu.HBM)],
-        out_specs=pl.BlockSpec(memory_space=pltpu.VMEM),
+        out_specs=pl.BlockSpec(memory_space=pl.ANY),
         scratch_shapes=[
             pltpu.VMEM((4, 2 * half), b16),
             pltpu.VMEM((1, half), f32),
@@ -252,13 +255,21 @@
             pltpu.VMEM((2, 128, 256), f32),
             pltpu.VMEM((2, tiles, 256), f32),
             pltpu.VMEM((2, 128, 256), f32),
-            pltpu.VMEM((16, 16, 256), f32),
             dma, dma, dma, dma((2,)), dma((2,)), dma((2,)), dma((2,)), dma((2,)), dma, dma,
         ],
         compiler_params=pltpu.CompilerParams(
-            collective_id=0, has_side_effects=True, vmem_limit_bytes=48 * 2**20),
+            collective_id=0, has_side_effects=True, vmem_limit_bytes=58 * 2**20),
         name="correlate",
     )(spectra, band_gain.reshape(1, half))
+    rows = pl.pallas_call(
+        assemble,
+        out_shape=jax.ShapeDtypeStruct((2 * MAXLAG + 1, 1, 256), f32),
+        in_specs=[pl.BlockSpec(memory_space=pltpu.VMEM)],
+        out_specs=pl.BlockSpec(memory_space=pltpu.VMEM),
+        scratch_shapes=[pltpu.VMEM((2, 128, 256), f32)],
+        name="assemble",
+    )(blocks)
+    return jnp.transpose(rows, (1, 0, 2))
 
 
 def solution(mesh):

time: 33.2 us -> 32.4 us (0.976)
  local copies, waits for them, and re-layouts: 2.35 us -> 0 us
  Pallas kernels: 30.7 us -> 32.2 us
    pallas_call x1 -> x2, Pallas kernels: 30.7 us -> 32.2 us  [the longest x1 30.4 us: body(): pl.pallas_call(kernel, out_shape=jax.ShapeDtypeStruct((16, 16, 256), f32)...]
    unnamed x4 -> x0, local copies, waits for them, and re-layouts: 1.45 us -> none
    pallas_call x1 -> x0, local copies, waits for them, and re-layouts: 0.89 us -> none  [body(): pl.pallas_call(kernel, out_shape=jax.ShapeDtypeStruct((1, 2 * MAXLAG + 1,...]
where the time goes in v3:
time: 32.4 us; the launch traced here: 32.3 us
  Pallas kernels  32.2 us (99%)
    pallas_call x1, Pallas kernels, body(): pl.pallas_call(kernel, out_shape=jax.ShapeDtypeStruct((16, 16, 256), f32)...  30.4 us
    pallas_call x1, Pallas kernels, body(): pl.pallas_call(assemble, out_shape=jax.ShapeDtypeStruct((2 * MAXLAG + 1,...  1.81 us

profile of v3, /device:TPU:1, one launch (start us, length us, event | category | flops | bytes accessed | tf_op | source)
XLA Modules:
  0.0 32.3 jit_solution(13966732802074039122)
XLA Ops:
  0.0 30.4 %correlate.1.rbuf = f32[16,16,256]{2,1,0:T(8,128)} custom-call(bf16[1,4,4096]{2,1,0:T(4,128)(2,1)} %x_ref.1, f32[1,2048]{1,0:T(1,128)} %bitcast.2), custom_call_target="tpu_custom_call" | custom-call | tf_op jit(solution)/shard_map/correlate/pallas_call | solution.py:239
  30.4 1.8 %assemble.1 = f32[201,1,256]{2,1,0:T(1,128)} custom-call(f32[16,16,256]{2,1,0:T(8,128)} %correlate.1.rbuf), custom_call_target="tpu_custom_call" | custom-call | tf_op jit(solution)/shard_map/assemble/pallas_call | solution.py:264

commit v4 on v3

--- a/solution.py
+++ b/solution.py
@@ -12,6 +12,7 @@
 MESH = pl.DeviceIdType.MESH
 BEHIND = [2, 3, 1, 0]
 STAGED = False
+ROWS = 8
 
 
 def place():
@@ -37,12 +38,11 @@
     pl.when(jnp.logical_not(condition))(no)
 
 
-def kernel(x_ref, g_ref, rbuf, own, gains, ibuf, jbuf, ifull, jfull, zh, zl, th, tl, base, steps,
+def kernel(x_ref, g_ref, rbuf, own, gains, ibuf, jbuf, ifull, jfull, zh, zl, wh, wl, steps,
            obuf, own_sem, gain_sem, isend, irecv, jsend, jrecv, ksend, krecv, osend, orecv):
     x, y, z, k = place()
     xh, xl = x // 2, lax.rem(x, 2)
     half = x_ref.shape[2] // 2
-    tiles = half // 128
     group = z // 4
 
     barrier = pltpu.get_barrier_semaphore()
@@ -68,16 +68,16 @@
 
     signal(device(x, y, z, 1 - k))
 
-    def phases(first, step, rows):
-        f = lax.broadcasted_iota(jnp.int32, (rows, 256), 0) * step + first
-        lag = lax.broadcasted_iota(jnp.int32, (rows, 256), 1) - MAXLAG
+    def phases(step, rows):
+        f = lax.broadcasted_iota(jnp.int32, (rows, 128), 0) * step
+        lag = lax.broadcasted_iota(jnp.int32, (rows, 128), 1)
         turn = jnp.bitwise_and(f * lag + half, 2 * half - 1) - half
         return turn.astype(jnp.float32) * (math.pi / half)
 
-    angle = phases(0, 1, 128)
-    base[0] = jnp.cos(angle)
-    base[1] = jnp.sin(angle)
-    angle = phases(0, 128, tiles)
+    angle = phases(1, 256)
+    wh[:, 0:128], wl[:, 0:128] = split(jnp.cos(angle))
+    wh[:, 128:256], wl[:, 128:256] = split(jnp.sin(angle))
+    angle = phases(256, half // 256)
     steps[0] = jnp.cos(angle)
     steps[1] = jnp.sin(angle)
 
@@ -123,12 +123,6 @@
     if not STAGED:
         ring_sends(1)
 
-    @pl.loop(0, tiles)
-    def _(t):
-        c, s = steps[0, pl.ds(t, 1), :], steps[1, pl.ds(t, 1), :]
-        th[t, 0:128], tl[t, 0:128] = split(base[0] * c - base[1] * s)
-        th[t, 128:256], tl[t, 128:256] = split(base[1] * c + base[0] * s)
-
     if STAGED:
         ring_left(0)
         ring_sends(1)
@@ -146,14 +140,15 @@
     scale = 1.0 / math.sqrt(half)
     my_o = y * 4 + x
 
-    for part in range(2):
-        here(ibuf.at[pl.ds(8 * part, 8)], irecv.at[part])
-
-        @pl.loop(0, 2)
+    for part in range(16 // ROWS):
+        if part * ROWS % 8 == 0:
+            here(ibuf.at[pl.ds(part * ROWS, 8)], irecv.at[part * ROWS // 8])
+
+        @pl.loop(0, ROWS // 4)
         def _(n, part=part):
             for s in range(4):
-                real = ibuf[8 * part + 4 * n + s, :, 0:half].astype(jnp.float32) * (gains[...] * scale)
-                imag = ibuf[8 * part + 4 * n + s, :, half:].astype(jnp.float32) * (gains[...] * scale)
+                real = ibuf[ROWS * part + 4 * n + s, :, 0:half].astype(jnp.float32) * (gains[...] * scale)
+                imag = ibuf[ROWS * part + 4 * n + s, :, half:].astype(jnp.float32) * (gains[...] * scale)
                 ifull[n, s, :, 0:half] = real
                 ifull[n, s, :, half:2 * half] = imag
                 ifull[n, s, :, 2 * half:] = real + imag
@@ -166,15 +161,16 @@
                     jfull[s, g] = jnp.concatenate([jbuf[s % 2, g, s // 2].astype(jnp.float32),
                                                    jbuf[s % 2, g, 2 + s // 2].astype(jnp.float32)], 0)
 
-        @pl.loop(0, tiles)
-        def _(t):
-            re = pl.ds(pl.multiple_of(t * 128, 128), 128)
-            im = pl.ds(pl.multiple_of(half + t * 128, 128), 128)
-            both = pl.ds(pl.multiple_of(2 * half + t * 128, 128), 128)
+        def cross(t, u):
+            offset = t * 256 + u * 128
+            re = pl.ds(pl.multiple_of(offset, 128), 128)
+            im = pl.ds(pl.multiple_of(half + offset, 128), 128)
+            both = pl.ds(pl.multiple_of(2 * half + offset, 128), 128)
+            cut = slice(u * 128, u * 128 + 128)
             jr = [[jfull[s, g, :, re] for g in range(2)] for s in range(4)]
             ji = [[jfull[s, g, :, im] for g in range(2)] for s in range(4)]
             jd = [[jr[s][g] - ji[s][g] for g in range(2)] for s in range(4)]
-            for i in range(8):
+            for i in range(ROWS):
                 ib = [ifull[i // 4, s, i % 4:i % 4 + 1, both] for s in range(4)]
                 ir = [ifull[i // 4, s, i % 4:i % 4 + 1, re] for s in range(4)]
                 ii = [ifull[i // 4, s, i % 4:i % 4 + 1, im] for s in range(4)]
@@ -185,18 +181,27 @@
                     bd = added([ib[s] * jd[s][g] for s in range(4)])
                     zr.append(rr + ss)
                     zi.append((rr - ss) - bd)
-                rows = slice(i * 16, i * 16 + 16)
-                zh[t, rows, 0:128], zl[t, rows, 0:128] = split(jnp.concatenate(zr, 0))
-                zh[t, rows, 128:256], zl[t, rows, 128:256] = split(jnp.concatenate(zi, 0))
-
-        total = None
-        for t in range(tiles):
-            term = dot(zh[t], th[t]) + dot(zl[t], th[t]) + dot(zh[t], tl[t])
-            total = term if total is None else total + term
-        obuf[part] = total
-
-        for n in range(8):
-            spot, r = 2 * part + n // 4, n % 4
+                for value, first in ((zr, 0), (zi, 16 * ROWS)):
+                    rows = slice(first + i * 16, first + i * 16 + 16)
+                    zh[t, rows, cut], zl[t, rows, cut] = split(jnp.concatenate(value, 0))
+
+        @pl.loop(0, half // 256)
+        def _(t, cross=cross):
+            for u in range(2):
+                cross(t, u)
+
+        even = odd = 0.0
+        edge = 16 * ROWS
+        for t in range(half // 256):
+            near = dot(zh[t], wh[...]) + dot(zl[t], wh[...]) + dot(zh[t], wl[...])
+            c, d = steps[0, t:t + 1, :], steps[1, t:t + 1, :]
+            even += c * near[0:edge, 0:128] - d * near[0:edge, 128:256]
+            odd += d * near[edge:, 0:128] + c * near[edge:, 128:256]
+        obuf[part, :, 0:128] = even + odd
+        obuf[part, :, 128:256] = even - odd
+
+        for n in range(ROWS):
+            spot, r = part * ROWS // 4 + n // 4, n % 4
             block = obuf.at[part, pl.ds(n * 16, 16)]
 
             def give(block=block, spot=spot, r=r):
@@ -220,7 +225,7 @@
     here(rbuf, orecv)
 
 
-def assemble(rbuf, out_ref, base):
+def assemble(rbuf, out_ref, base, turned):
     for b in range(8):
         rows = []
         for m in range(4):
@@ -228,12 +233,15 @@
         base[b // 4, (b % 4) * 32:(b % 4) * 32 + 32, :] = jnp.concatenate(rows, 0)
 
     for h in range(2):
-        out_ref[:, 0, h * 128:(h + 1) * 128] = base[h].T[0:2 * MAXLAG + 1]
+        cut = slice(h * 128, (h + 1) * 128)
+        turned[...] = base[h].T
+        out_ref[MAXLAG:, 0, cut] = turned[0:MAXLAG + 1]
+        for lag in range(1, MAXLAG + 1):
+            out_ref[MAXLAG - lag:MAXLAG - lag + 1, 0, cut] = turned[128 + lag:129 + lag]
 
 
 def body(spectra, band_gain):
     half = band_gain.shape[0]
-    tiles = half // 128
     f32, b16 = jnp.float32, jnp.bfloat16
     dma = pltpu.SemaphoreType.DMA
     blocks = pl.pallas_call(
@@ -248,13 +256,12 @@
             pltpu.VMEM((2, 2, 4, 4, 2 * half), b16),
             pltpu.VMEM((2, 4, 4, 3 * half), f32),
             pltpu.VMEM((4, 2, 8, 2 * half), f32),
-            pltpu.VMEM((tiles, 128, 256), b16),
-            pltpu.VMEM((tiles, 128, 256), b16),
-            pltpu.VMEM((tiles, 256, 256), b16),
-            pltpu.VMEM((tiles, 256, 256), b16),
-            pltpu.VMEM((2, 128, 256), f32),
-            pltpu.VMEM((2, tiles, 256), f32),
-            pltpu.VMEM((2, 128, 256), f32),
+            pltpu.VMEM((half // 256, 32 * ROWS, 256), b16),
+            pltpu.VMEM((half // 256, 32 * ROWS, 256), b16),
+            pltpu.VMEM((256, 256), b16),
+            pltpu.VMEM((256, 256), b16),
+            pltpu.VMEM((2, half // 256, 128), f32),
+            pltpu.VMEM((16 // ROWS, 16 * ROWS, 256), f32),
             dma, dma, dma, dma((2,)), dma((2,)), dma((2,)), dma((2,)), dma((2,)), dma, dma,
         ],
         compiler_params=pltpu.CompilerParams(
@@ -266,7 +273,7 @@
         out_shape=jax.ShapeDtypeStruct((2 * MAXLAG + 1, 1, 256), f32),
         in_specs=[pl.BlockSpec(memory_space=pltpu.VMEM)],
         out_specs=pl.BlockSpec(memory_space=pltpu.VMEM),
-        scratch_shapes=[pltpu.VMEM((2, 128, 256), f32)],
+        scratch_shapes=[pltpu.VMEM((2, 128, 256), f32), pltpu.VMEM((256, 128), f32)],
         name="assemble",
     )(blocks)
     return jnp.transpose(rows, (1, 0, 2))

time: 32.4 us -> 30.6 us (0.944)
  Pallas kernels: 32.2 us -> 30.5 us
    pallas_call x1, Pallas kernels: 30.4 us -> 28.6 us  [body(): pl.pallas_call(kernel, out_shape=jax.ShapeDtypeStruct((16, 16, 256), f32)...]
where the time goes in v4:
time: 30.6 us; the launch traced here: 30.5 us
  Pallas kernels  30.5 us (100%)
    pallas_call x1, Pallas kernels, body(): pl.pallas_call(kernel, out_shape=jax.ShapeDtypeStruct((16, 16, 256), f32)...  28.6 us
    pallas_call x1, Pallas kernels, body(): pl.pallas_call(assemble, out_shape=jax.ShapeDtypeStruct((2 * MAXLAG + 1,...  1.84 us

profile of v4, /device:TPU:1, one launch (start us, length us, event | category | flops | bytes accessed | tf_op | source)
XLA Modules:
  0.0 30.5 jit_solution(5447170727808575192)
XLA Ops:
  0.0 28.6 %correlate.1.rbuf = f32[16,16,256]{2,1,0:T(8,128)} custom-call(bf16[1,4,4096]{2,1,0:T(4,128)(2,1)} %x_ref.1, f32[1,2048]{1,0:T(1,128)} %bitcast.2), custom_call_target="tpu_custom_call" | custom-call | tf_op jit(solution)/shard_map/correlate/pallas_call | solution.py:247
  28.6 1.8 %assemble.1 = f32[201,1,256]{2,1,0:T(1,128)} custom-call(f32[16,16,256]{2,1,0:T(8,128)} %correlate.1.rbuf), custom_call_target="tpu_custom_call" | custom-call | tf_op jit(solution)/shard_map/assemble/pallas_call | solution.py:271

commit v5 on v4

--- a/solution.py
+++ b/solution.py
@@ -30,7 +30,7 @@
 
 
 def added(terms):
-    return (terms[0] + terms[1]) + (terms[2] + terms[3])
+    return sum(terms[1:], terms[0]) if len(terms) < 4 else (terms[0] + terms[1]) + (terms[2] + terms[3])
 
 
 def either(condition, yes, no):
@@ -38,7 +38,7 @@
     pl.when(jnp.logical_not(condition))(no)
 
 
-def kernel(x_ref, g_ref, rbuf, own, gains, ibuf, jbuf, ifull, jfull, zh, zl, wh, wl, steps,
+def kernel(x_ref, g_ref, rbuf, own, gains, ibuf, jbuf, ifull, jfull, zfirst, zh, zl, wh, wl, steps,
            obuf, own_sem, gain_sem, isend, irecv, jsend, jrecv, ksend, krecv, osend, orecv):
     x, y, z, k = place()
     xh, xl = x // 2, lax.rem(x, 2)
@@ -93,11 +93,11 @@
     def ring_sends(g):
         @pl.loop(0, 4)
         def _(n):
-            tz = g * 4 + lax.rem(z + 2 + n, 4)
+            tz = g * 4 + n
             either(j_self & (tz == z),
-                   lambda: pltpu.make_async_copy(own, jbuf.at[k, group, my_j], jrecv.at[group]).start(),
+                   lambda: pltpu.make_async_copy(own, jbuf.at[k, group, my_j], jrecv.at[group * 4 + my_j]).start(),
                    lambda: pltpu.make_async_remote_copy(
-                       own, jbuf.at[k, group, my_j], jsend.at[g], jrecv.at[group],
+                       own, jbuf.at[k, group, my_j], jsend.at[g], jrecv.at[group * 4 + my_j],
                        device_id=device(xh * 2 + lax.rem(z, 2), y, tz, k), device_id_type=MESH).start())
 
     def plane_send(dx, dy):
@@ -132,9 +132,10 @@
 
     for turn in range(2):
         g = group if turn == 0 else 1 - group
-        here(jbuf.at[k, g], jrecv.at[g])
-        pltpu.make_async_remote_copy(jbuf.at[k, g], jbuf.at[k, g], ksend.at[g], krecv.at[g],
-                                     device_id=device(x, y, z, 1 - k), device_id_type=MESH).start()
+        for n in range(4):
+            here(jbuf.at[k, g, n], jrecv.at[g * 4 + n])
+            pltpu.make_async_remote_copy(jbuf.at[k, g, n], jbuf.at[k, g, n], ksend, krecv.at[g],
+                                         device_id=device(x, y, z, 1 - k), device_id_type=MESH).start()
 
     dot = functools.partial(jnp.dot, preferred_element_type=jnp.float32)
     scale = 1.0 / math.sqrt(half)
@@ -153,42 +154,50 @@
                 ifull[n, s, :, half:2 * half] = imag
                 ifull[n, s, :, 2 * half:] = real + imag
 
-        if part == 0:
-            for g in range(2):
-                here(jbuf.at[1 - k, g], krecv.at[g])
-            for s in range(4):
-                for g in range(2):
-                    jfull[s, g] = jnp.concatenate([jbuf[s % 2, g, s // 2].astype(jnp.float32),
-                                                   jbuf[s % 2, g, 2 + s // 2].astype(jnp.float32)], 0)
-
-        def cross(t, u):
+        def cross(t, u, segments, turn):
             offset = t * 256 + u * 128
             re = pl.ds(pl.multiple_of(offset, 128), 128)
             im = pl.ds(pl.multiple_of(half + offset, 128), 128)
             both = pl.ds(pl.multiple_of(2 * half + offset, 128), 128)
             cut = slice(u * 128, u * 128 + 128)
-            jr = [[jfull[s, g, :, re] for g in range(2)] for s in range(4)]
-            ji = [[jfull[s, g, :, im] for g in range(2)] for s in range(4)]
-            jd = [[jr[s][g] - ji[s][g] for g in range(2)] for s in range(4)]
+            jr = [[jfull[s, g, :, re] for g in range(2)] for s in segments]
+            ji = [[jfull[s, g, :, im] for g in range(2)] for s in segments]
+            jd = [[p[g] - q[g] for g in range(2)] for p, q in zip(jr, ji)]
             for i in range(ROWS):
-                ib = [ifull[i // 4, s, i % 4:i % 4 + 1, both] for s in range(4)]
-                ir = [ifull[i // 4, s, i % 4:i % 4 + 1, re] for s in range(4)]
-                ii = [ifull[i // 4, s, i % 4:i % 4 + 1, im] for s in range(4)]
+                ib = [ifull[i // 4, s, i % 4:i % 4 + 1, both] for s in segments]
+                ir = [ifull[i // 4, s, i % 4:i % 4 + 1, re] for s in segments]
+                ii = [ifull[i // 4, s, i % 4:i % 4 + 1, im] for s in segments]
                 zr, zi = [], []
                 for g in range(2):
-                    rr = added([ir[s] * jr[s][g] for s in range(4)])
-                    ss = added([ii[s] * ji[s][g] for s in range(4)])
-                    bd = added([ib[s] * jd[s][g] for s in range(4)])
+                    rr = added([p * q[g] for p, q in zip(ir, jr)])
+                    ss = added([p * q[g] for p, q in zip(ii, ji)])
+                    bd = added([p * q[g] for p, q in zip(ib, jd)])
                     zr.append(rr + ss)
                     zi.append((rr - ss) - bd)
                 for value, first in ((zr, 0), (zi, 16 * ROWS)):
                     rows = slice(first + i * 16, first + i * 16 + 16)
-                    zh[t, rows, cut], zl[t, rows, cut] = split(jnp.concatenate(value, 0))
-
-        @pl.loop(0, half // 256)
-        def _(t, cross=cross):
-            for u in range(2):
-                cross(t, u)
+                    value = jnp.concatenate(value, 0)
+                    if turn == 0:
+                        zfirst[t, rows, cut] = value
+                    else:
+                        zh[t, rows, cut], zl[t, rows, cut] = split(zfirst[t, rows, cut] + value if turn == 1 else value)
+
+        for turn in ((0, 1) if part == 0 else (2,)):
+            core = k if turn == 0 else 1 - k
+            if turn == 1:
+                for g in range(2):
+                    here(jbuf.at[1 - k, g], krecv.at[g])
+            if turn < 2:
+                for a in range(2):
+                    for g in range(2):
+                        jfull[2 * a + core, g] = jnp.concatenate([jbuf[core, g, a].astype(jnp.float32),
+                                                                  jbuf[core, g, 2 + a].astype(jnp.float32)], 0)
+            segments = (core, 2 + core) if turn < 2 else (0, 1, 2, 3)
+
+            @pl.loop(0, half // 256)
+            def _(t, cross=cross, segments=segments, turn=turn):
+                for u in range(2):
+                    cross(t, u, segments, turn)
 
         even = odd = 0.0
         edge = 16 * ROWS
@@ -219,8 +228,7 @@
 
     for g in range(1 if STAGED else 0, 2):
         ring_left(g)
-    for g in range(2):
-        pltpu.make_async_copy(jbuf.at[0, g], jbuf.at[0, g], ksend.at[g]).wait()
+    here(jbuf.at[0], ksend)
 
     here(rbuf, orecv)
 
@@ -256,13 +264,14 @@
             pltpu.VMEM((2, 2, 4, 4, 2 * half), b16),
             pltpu.VMEM((2, 4, 4, 3 * half), f32),
             pltpu.VMEM((4, 2, 8, 2 * half), f32),
+            pltpu.VMEM((half // 256, 32 * ROWS, 256), f32),
             pltpu.VMEM((half // 256, 32 * ROWS, 256), b16),
             pltpu.VMEM((half // 256, 32 * ROWS, 256), b16),
             pltpu.VMEM((256, 256), b16),
             pltpu.VMEM((256, 256), b16),
             pltpu.VMEM((2, half // 256, 128), f32),
             pltpu.VMEM((16 // ROWS, 16 * ROWS, 256), f32),
-            dma, dma, dma, dma((2,)), dma((2,)), dma((2,)), dma((2,)), dma((2,)), dma, dma,
+            dma, dma, dma, dma((2,)), dma((2,)), dma((8,)), dma, dma((2,)), dma, dma,
         ],
         compiler_params=pltpu.CompilerParams(
             collective_id=0, has_side_effects=True, vmem_limit_bytes=58 * 2**20),

time: 30.6 us -> 30.5 us (level)
  no operation moved by 1% of the time
where the time goes in v5:
time: 30.5 us; the launch traced here: 30.4 us
  Pallas kernels  30.4 us (100%)
    pallas_call x1, Pallas kernels, body(): pl.pallas_call(kernel, out_shape=jax.ShapeDtypeStruct((16, 16, 256), f32)...  28.5 us
    pallas_call x1, Pallas kernels, body(): pl.pallas_call(assemble, out_shape=jax.ShapeDtypeStruct((2 * MAXLAG + 1,...  1.84 us

profile of v5, /device:TPU:1, one launch (start us, length us, event | category | flops | bytes accessed | tf_op | source)
XLA Modules:
  0.0 30.4 jit_solution(15933774675031141375)
XLA Ops:
  0.0 28.5 %correlate.1.rbuf = f32[16,16,256]{2,1,0:T(8,128)} custom-call(bf16[1,4,4096]{2,1,0:T(4,128)(2,1)} %x_ref.1, f32[1,2048]{1,0:T(1,128)} %bitcast.2), custom_call_target="tpu_custom_call" | custom-call | tf_op jit(solution)/shard_map/correlate/pallas_call | solution.py:255
  28.6 1.8 %assemble.1 = f32[201,1,256]{2,1,0:T(1,128)} custom-call(f32[16,16,256]{2,1,0:T(8,128)} %correlate.1.rbuf), custom_call_target="tpu_custom_call" | custom-call | tf_op jit(solution)/shard_map/assemble/pallas_call | solution.py:280

commit v6 on v4

--- a/solution.py
+++ b/solution.py
@@ -12,7 +12,7 @@
 MESH = pl.DeviceIdType.MESH
 BEHIND = [2, 3, 1, 0]
 STAGED = False
-ROWS = 8
+ROWS = 4
 
 
 def place():
@@ -102,7 +102,7 @@
 
     def plane_send(dx, dy):
         spot = BEHIND.index((4 - dy) % 4)
-        pltpu.make_async_remote_copy(own, ibuf.at[spot * 4 + my_seg], isend, irecv.at[spot // 2],
+        pltpu.make_async_remote_copy(own, ibuf.at[spot * 4 + my_seg], isend, irecv.at[spot],
                                      device_id=device(lax.rem(x + dx, 4), lax.rem(y + dy, 4), z, xh), device_id_type=MESH).start()
 
     def left(ref, sem):
@@ -119,7 +119,7 @@
         if dy:
             plane_send(0, dy)
         else:
-            either(i_self, lambda: pltpu.make_async_copy(own, ibuf.at[12 + my_seg], irecv.at[1]).start(), lambda: plane_send(0, 0))
+            either(i_self, lambda: pltpu.make_async_copy(own, ibuf.at[12 + my_seg], irecv.at[3]).start(), lambda: plane_send(0, 0))
     if not STAGED:
         ring_sends(1)
 
@@ -141,8 +141,7 @@
     my_o = y * 4 + x
 
     for part in range(16 // ROWS):
-        if part * ROWS % 8 == 0:
-            here(ibuf.at[pl.ds(part * ROWS, 8)], irecv.at[part * ROWS // 8])
+        here(ibuf.at[pl.ds(part * ROWS, ROWS)], irecv.at[part])
 
         @pl.loop(0, ROWS // 4)
         def _(n, part=part):
@@ -262,7 +261,7 @@
             pltpu.VMEM((256, 256), b16),
             pltpu.VMEM((2, half // 256, 128), f32),
             pltpu.VMEM((16 // ROWS, 16 * ROWS, 256), f32),
-            dma, dma, dma, dma((2,)), dma((2,)), dma((2,)), dma((2,)), dma((2,)), dma, dma,
+            dma, dma, dma, dma((4,)), dma((2,)), dma((2,)), dma((2,)), dma((2,)), dma, dma,
         ],
         compiler_params=pltpu.CompilerParams(
             collective_id=0, has_side_effects=True, vmem_limit_bytes=58 * 2**20),

time: 30.6 us -> 30.2 us (0.987)
  Pallas kernels: 30.5 us -> 30.1 us
    pallas_call x1, Pallas kernels: 28.6 us -> 28.3 us  [body(): pl.pallas_call(kernel, out_shape=jax.ShapeDtypeStruct((16, 16, 256), f32)...]
where the time goes in v6:
time: 30.2 us; the launch traced here: 30.1 us
  Pallas kernels  30.1 us (100%)
    pallas_call x1, Pallas kernels, body(): pl.pallas_call(kernel, out_shape=jax.ShapeDtypeStruct((16, 16, 256), f32)...  28.3 us
    pallas_call x1, Pallas kernels, body(): pl.pallas_call(assemble, out_shape=jax.ShapeDtypeStruct((2 * MAXLAG + 1,...  1.84 us

profile of v6, /device:TPU:1, one launch (start us, length us, event | category | flops | bytes accessed | tf_op | source)
XLA Modules:
  0.0 30.1 jit_solution(14280884014559496882)
XLA Ops:
  0.0 28.3 %correlate.1.rbuf = f32[16,16,256]{2,1,0:T(8,128)} custom-call(bf16[1,4,4096]{2,1,0:T(4,128)(2,1)} %x_ref.1, f32[1,2048]{1,0:T(1,128)} %bitcast.2), custom_call_target="tpu_custom_call" | custom-call | tf_op jit(solution)/shard_map/correlate/pallas_call | solution.py:246
  28.3 1.8 %assemble.1 = f32[201,1,256]{2,1,0:T(1,128)} custom-call(f32[16,16,256]{2,1,0:T(8,128)} %correlate.1.rbuf), custom_call_target="tpu_custom_call" | custom-call | tf_op jit(solution)/shard_map/assemble/pallas_call | solution.py:270

commit v7 on v6

--- a/solution.py
+++ b/solution.py
@@ -93,7 +93,7 @@
     def ring_sends(g):
         @pl.loop(0, 4)
         def _(n):
-            tz = g * 4 + lax.rem(z + 2 + n, 4)
+            tz = g * 4 + n
             either(j_self & (tz == z),
                    lambda: pltpu.make_async_copy(own, jbuf.at[k, group, my_j], jrecv.at[group]).start(),
                    lambda: pltpu.make_async_remote_copy(

time: 30.2 us -> 29.2 us (0.967)
  Pallas kernels: 30.1 us -> 29.1 us
    pallas_call x1, Pallas kernels: 28.3 us -> 27.2 us  [body(): pl.pallas_call(kernel, out_shape=jax.ShapeDtypeStruct((16, 16, 256), f32)...]
where the time goes in v7:
time: 29.2 us; the launch traced here: 29.1 us
  Pallas kernels  29.1 us (100%)
    pallas_call x1, Pallas kernels, body(): pl.pallas_call(kernel, out_shape=jax.ShapeDtypeStruct((16, 16, 256), f32)...  27.2 us
    pallas_call x1, Pallas kernels, body(): pl.pallas_call(assemble, out_shape=jax.ShapeDtypeStruct((2 * MAXLAG + 1,...  1.84 us

profile of v7, /device:TPU:1, one launch (start us, length us, event | category | flops | bytes accessed | tf_op | source)
XLA Modules:
  0.0 29.1 jit_solution(12838694779607535256)
XLA Ops:
  0.0 27.2 %correlate.1.rbuf = f32[16,16,256]{2,1,0:T(8,128)} custom-call(bf16[1,4,4096]{2,1,0:T(4,128)(2,1)} %x_ref.1, f32[1,2048]{1,0:T(1,128)} %bitcast.2), custom_call_target="tpu_custom_call" | custom-call | tf_op jit(solution)/shard_map/correlate/pallas_call | solution.py:246
  27.2 1.8 %assemble.1 = f32[201,1,256]{2,1,0:T(1,128)} custom-call(f32[16,16,256]{2,1,0:T(8,128)} %correlate.1.rbuf), custom_call_target="tpu_custom_call" | custom-call | tf_op jit(solution)/shard_map/assemble/pallas_call | solution.py:270
